TPU v7x, 128 devices: a whole 4x4x4 slice. The times are simulated.
128 devices in a mesh: dp: 16 (over z, y), ctx: 2 (over core), tensor: 4 (over x).
Axes of the slice: x: 4, y: 4, z: 4, core: 2. Of those that a mesh axis runs over, the one named last changes fastest.
Arguments:
- patches: bfloat16 [30720, 768], P(('dp', 'ctx')), may hold values from -6 to 6
- text_features: bfloat16 [64, 16, 768], P('dp', 'ctx'), may hold values from -6 to 6
- patch_weight: bfloat16 [768, 768], P(None, 'tensor'), may hold values from -0.21875 to 0.21875
- patch_bias: float32 [768], P('tensor'), may hold values from -3 to 3
- text_weight: bfloat16 [768, 768], P(None, 'tensor'), may hold values from -0.21875 to 0.21875
- text_bias: float32 [768], P('tensor'), may hold values from -3 to 3
- readout: bfloat16 [768], P('tensor'), may hold values from -6 to 6
- mix_gain: float32 [2, 768], replicated, may hold values from 0.5 to 1.5
- mix_shift: float32 [2, 768], replicated, may hold values from -2 to 2
- heads_in_weight: bfloat16 [2, 768, 3, 768], P(None, None, None, 'tensor'), may hold values from -0.21875 to 0.21875
- heads_out_weight: bfloat16 [2, 768, 768], P(None, 'tensor'), may hold values from -3 to 3
- feed_gain: float32 [2, 768], replicated, may hold values from 0.5 to 1.5
- feed_shift: float32 [2, 768], replicated, may hold values from -2 to 2
- up_weight: bfloat16 [2, 768, 3072], P(None, None, 'tensor'), may hold values from -0.21875 to 0.21875
- up_bias: float32 [2, 3072], P(None, 'tensor'), may hold values from -3 to 3
- down_weight: bfloat16 [2, 3072, 768], P(None, 'tensor'), may hold values from -0.109375 to 0.109375
- timesteps: int32 [64, 512], P('dp'), may hold values from 0 to 15, as said below
- datasets: int32 [64], P('dp'), may hold values from 0 to 24
- dataset_weights: int32 [25], replicated, may hold values from 1 to 4
- action_mask: int32 [64, 16], P('dp', 'ctx'), may hold values 0 or 1
- cotangent: bfloat16 [64, 512, 768], P('dp', 'ctx'), may hold values from -6 to 6
Outputs:
- activations: bfloat16 [64, 512, 768], P('dp', 'ctx', 'tensor')
- patches_gradient: float32 [30720, 768], P(('dp', 'ctx'), 'tensor')
- text_gradient: float32 [64, 16, 768], P('dp', 'ctx', 'tensor')
- patch_weight_gradient: float32 [768, 768], P(None, 'tensor')
- patch_bias_gradient: float32 [768], P('tensor')
- text_weight_gradient: float32 [768, 768], P(None, 'tensor')
- text_bias_gradient: float32 [768], P('tensor')
- readout_gradient: float32 [768], P('tensor')
- mix_gain_gradient: float32 [2, 768], P(None, 'tensor')
- mix_shift_gradient: float32 [2, 768], P(None, 'tensor')
- heads_in_gradient: float32 [2, 768, 3, 768], P(None, None, None, 'tensor')
- heads_out_gradient: float32 [2, 768, 768], P(None, 'tensor')
- feed_gain_gradient: float32 [2, 768], P(None, 'tensor')
- feed_shift_gradient: float32 [2, 768], P(None, 'tensor')
- up_weight_gradient: float32 [2, 768, 3072], P(None, None, 'tensor')
- up_bias_gradient: float32 [2, 3072], P(None, 'tensor')
- down_weight_gradient: float32 [2, 3072, 768], P(None, 'tensor')
Inputs may be any that keep to these rules, and one draw needn't show every extreme that they name: `timesteps`: each item's row starts at 0 and never falls, rising by 0 or 1 from one position to the next and ending at the maximum; positions 192 to 320 share one value.
All inputs are finite; a program needn't handle non-finite values. No bound on the sum of `action_mask` on one device may be relied on, other than what follows from the above.
Results may differ from a plain program's by a relative error of at most 0.028.
Values may be sent and summed in bfloat16 or wider, within the bound.
A program may use at most 192 MiB of HBM per device.

v0:
```python
import jax
import jax.numpy as jnp
from jax import lax
from jax.sharding import PartitionSpec as P

HEAD_DIM = 64
NL = 2
L = 512
IMG_GROUP = 30


EPS = 1e-06
MASKED = -1e30


def normalize(stream, gain_row, shift_row):
    row_mean = jnp.mean(stream, axis=-1, keepdims=True)
    centred = stream - row_mean
    spread = jnp.mean(centred * centred, axis=-1, keepdims=True)
    return centred * lax.rsqrt(spread + EPS) * gain_row + shift_row


def smooth(pre_act):
    return jax.nn.gelu(pre_act, approximate=True)


def shards(
    patches,
    text_features,
    patch_weight,
    patch_bias,
    text_weight,
    text_bias,
    readout,
    mix_gain,
    mix_shift,
    heads_in_weight,
    heads_out_weight,
    feed_gain,
    feed_shift,
    up_weight,
    up_bias,
    down_weight,
    timesteps,
    datasets,
    dataset_weights,
    action_mask,
    cotangent,
):
    seqs, half, width = cotangent.shape
    half_groups = text_features.shape[1]
    width_dev = patch_weight.shape[1]
    heads_dev = width_dev // HEAD_DIM
    rows = seqs * half
    group = IMG_GROUP + 2
    scale = HEAD_DIM ** (-0.5)
    column = lax.axis_index("tensor") * width_dev
    stamps_query = lax.dynamic_slice_in_dim(timesteps, lax.axis_index("ctx") * half, half, 1)
    visible = timesteps[:, None, None, :] <= stamps_query[:, None, :, None]

    def own_slice(vector):
        return lax.dynamic_slice_in_dim(vector, column, width_dev, 0)

    def split_heads(array, length):
        return array.reshape(seqs, length, heads_dev, HEAD_DIM)

    def project_heads(normed, which):
        triple = jnp.einsum(
            "rd,dcn->rcn", normed, heads_in_weight[which], preferred_element_type=jnp.float32
        ).astype(jnp.bfloat16)
        queries = triple[:, 0].reshape(seqs, half, width_dev)
        keys_own = triple[:, 1].reshape(seqs, half, width_dev)
        values_own = triple[:, 2].reshape(seqs, half, width_dev)
        return (queries, keys_own, values_own)

    def scores_of(queries, keys_all):
        raw = (
            jnp.einsum(
                "bqhd,bkhd->bhqk",
                split_heads(queries, half),
                split_heads(keys_all, L),
                preferred_element_type=jnp.float32,
            )
            * scale
        )
        return jnp.where(visible, raw, MASKED)

    def mix_values(probs_low, values_all):
        mixed = jnp.einsum(
            "bhqk,bkhd->bqhd",
            probs_low,
            split_heads(values_all, L),
            preferred_element_type=jnp.float32,
        )
        return mixed.astype(jnp.bfloat16).reshape(rows, width_dev)

    def feed_inputs(feed_normed, which):
        pre_act = (
            jnp.dot(feed_normed, up_weight[which], preferred_element_type=jnp.float32)
            + up_bias[which]
        )
        return (pre_act, smooth(pre_act).astype(jnp.bfloat16))

    def layer_backward(stream, middle, normed, feed_normed, log_total, upstream, which):
        queries, keys_own, values_own = project_heads(normed, which)
        keys_all, values_all = (
            lax.all_gather(keys_own, "ctx", axis=1, tiled=True),
            lax.all_gather(values_own, "ctx", axis=1, tiled=True),
        )
        probs = jnp.exp(scores_of(queries, keys_all) - log_total)
        probs_low = probs.astype(jnp.bfloat16)
        mixed = mix_values(probs_low, values_all)
        pre_act, hidden = feed_inputs(feed_normed, which)
        upstream_low = upstream.astype(jnp.bfloat16)
        down_gradient = jnp.einsum(
            "rf,rd->fd", hidden, upstream_low, preferred_element_type=jnp.float32
        )
        hidden_gradient = jnp.einsum(
            "rd,fd->rf", upstream_low, down_weight[which], preferred_element_type=jnp.float32
        )
        pre_gradient = jax.vjp(smooth, pre_act)[1](hidden_gradient)[0].astype(jnp.bfloat16)
        up_gradient = jnp.einsum(
            "rd,rf->df", feed_normed, pre_gradient, preferred_element_type=jnp.float32
        )
        up_bias_gradient = jnp.sum(pre_gradient.astype(jnp.float32), axis=0)
        feed_terms = jnp.einsum(
            "rf,df->rd", pre_gradient, up_weight[which], preferred_element_type=jnp.float32
        )
        feed_back = lax.psum(feed_terms.astype(jnp.bfloat16), "tensor").astype(jnp.float32)
        feed_pull = jax.vjp(normalize, middle, feed_gain[which], feed_shift[which])[1]
        middle_part, feed_gain_gradient, feed_shift_gradient = feed_pull(feed_back)
        middle_gradient = upstream + middle_part
        middle_low = middle_gradient.astype(jnp.bfloat16)
        out_gradient = jnp.einsum(
            "rn,rd->nd", mixed, middle_low, preferred_element_type=jnp.float32
        )
        mixed_gradient = jnp.einsum(
            "rd,nd->rn", middle_low, heads_out_weight[which], preferred_element_type=jnp.float32
        ).astype(jnp.bfloat16)
        mixed_heads = split_heads(mixed_gradient, half)
        prob_gradient = jnp.einsum(
            "bqhd,bkhd->bhqk",
            mixed_heads,
            split_heads(values_all, L),
            preferred_element_type=jnp.float32,
        )
        score_gradient = probs * (
            prob_gradient - jnp.sum(probs * prob_gradient, axis=-1, keepdims=True)
        )
        score_gradient = score_gradient.astype(jnp.bfloat16)
        query_gradient = (
            jnp.einsum(
                "bhqk,bkhd->bqhd",
                score_gradient,
                split_heads(keys_all, L),
                preferred_element_type=jnp.float32,
            )
            * scale
        )
        key_terms = (
            jnp.einsum(
                "bhqk,bqhd->bkhd",
                score_gradient,
                split_heads(queries, half),
                preferred_element_type=jnp.float32,
            )
            * scale
        )
        value_terms = jnp.einsum(
            "bhqk,bqhd->bkhd", probs_low, mixed_heads, preferred_element_type=jnp.float32
        )
        key_gradient, value_gradient = (
            lax.psum_scatter(
                key_terms.reshape(seqs, L, width_dev).astype(jnp.bfloat16),
                "ctx",
                scatter_dimension=1,
                tiled=True,
            ).astype(jnp.float32),
            lax.psum_scatter(
                value_terms.reshape(seqs, L, width_dev).astype(jnp.bfloat16),
                "ctx",
                scatter_dimension=1,
                tiled=True,
            ).astype(jnp.float32),
        )
        triple_gradient = jnp.stack(
            [
                query_gradient.astype(jnp.bfloat16).reshape(rows, width_dev),
                key_gradient.astype(jnp.bfloat16).reshape(rows, width_dev),
                value_gradient.astype(jnp.bfloat16).reshape(rows, width_dev),
            ],
            axis=1,
        )
        in_gradient = jnp.einsum(
            "rd,rcn->dcn", normed, triple_gradient, preferred_element_type=jnp.float32
        )
        mix_terms = jnp.einsum(
            "rcn,dcn->rd",
            triple_gradient,
            heads_in_weight[which],
            preferred_element_type=jnp.float32,
        )
        mix_back = lax.psum(mix_terms.astype(jnp.bfloat16), "tensor").astype(jnp.float32)
        mix_pull = jax.vjp(normalize, stream, mix_gain[which], mix_shift[which])[1]
        stream_part, mix_gain_gradient, mix_shift_gradient = mix_pull(mix_back)
        gains = (
            own_slice(mix_gain_gradient),
            own_slice(mix_shift_gradient),
            own_slice(feed_gain_gradient),
            own_slice(feed_shift_gradient),
        )
        results = [
            gains[0],
            gains[1],
            in_gradient,
            out_gradient,
            gains[2],
            gains[3],
            up_gradient,
            up_bias_gradient,
            down_gradient,
        ]
        return (middle_gradient + stream_part, results)

    picture = (
        jnp.dot(patches, patch_weight, preferred_element_type=jnp.float32) + patch_bias
    ).astype(jnp.bfloat16)
    text_flat = text_features.reshape(seqs * half_groups, text_features.shape[2])
    words = (
        jnp.dot(text_flat, text_weight, preferred_element_type=jnp.float32) + text_bias
    ).astype(jnp.bfloat16)
    arrived = lax.all_to_all(picture, "dp", split_axis=0, concat_axis=0, tiled=True)
    picture_full, words_full, marker_full = (
        lax.all_gather(arrived, "tensor", axis=1, tiled=True),
        lax.all_gather(words, "tensor", axis=1, tiled=True),
        lax.all_gather(readout, "tensor", axis=0, tiled=True),
    )
    picture_full = picture_full.reshape(seqs, half_groups, IMG_GROUP, width)
    words_full = words_full.reshape(seqs, half_groups, 1, width)
    marker_full = jnp.broadcast_to(marker_full, (seqs, half_groups, 1, width))
    stream = (
        jnp.concatenate([picture_full, words_full, marker_full], axis=2)
        .astype(jnp.float32)
        .reshape(rows, width)
    )
    inputs_kept = []
    middles = []
    normeds = []
    feed_normeds = []
    pairs = []
    totals = []
    for which in range(NL):
        inputs_kept.append(stream)
        layer_normed = normalize(stream, mix_gain[which], mix_shift[which]).astype(jnp.bfloat16)
        layer_queries, layer_keys_own, layer_values_own = project_heads(layer_normed, which)
        layer_keys_all = lax.all_gather(layer_keys_own, "ctx", axis=1, tiled=True)
        layer_values_all = lax.all_gather(layer_values_own, "ctx", axis=1, tiled=True)
        scores = scores_of(layer_queries, layer_keys_all)
        top = jnp.max(scores, axis=-1, keepdims=True)
        weights = jnp.exp(scores - top)
        total = jnp.sum(weights, axis=-1, keepdims=True)
        layer_probs = weights / total
        layer_log_total = top + jnp.log(total)
        layer_mixed = mix_values(layer_probs.astype(jnp.bfloat16), layer_values_all)
        layer_mix_terms = jnp.dot(
            layer_mixed, heads_out_weight[which], preferred_element_type=jnp.float32
        )
        branch = lax.psum(layer_mix_terms.astype(jnp.bfloat16), "tensor").astype(jnp.float32)
        layer_middle = stream + branch
        layer_feed_normed = normalize(layer_middle, feed_gain[which], feed_shift[which]).astype(
            jnp.bfloat16
        )
        layer_pre_act, layer_hidden = feed_inputs(layer_feed_normed, which)
        layer_feed_terms = jnp.dot(
            layer_hidden, down_weight[which], preferred_element_type=jnp.float32
        )
        branch_two = lax.psum(layer_feed_terms.astype(jnp.bfloat16), "tensor").astype(jnp.float32)
        stream = layer_middle + branch_two
        middle = layer_middle
        normed = layer_normed
        feed_normed = layer_feed_normed
        pair = (layer_keys_all, layer_values_all)
        log_total = layer_log_total
        middles.append(middle)
        normeds.append(normed)
        feed_normeds.append(feed_normed)
        pairs.append(pair)
        totals.append(log_total)
    activations = (
        lax.dynamic_slice_in_dim(stream, column, width_dev, 1)
        .astype(jnp.bfloat16)
        .reshape(seqs, half, width_dev)
    )
    chosen = datasets[:, None] == jnp.arange(dataset_weights.shape[0])[None, :]
    item_weight = jnp.sum(jnp.where(chosen, dataset_weights[None, :], 0), axis=1).astype(
        jnp.float32
    )
    readout_scale = item_weight[:, None] * action_mask.astype(jnp.float32)
    upstream = cotangent.astype(jnp.float32).reshape(seqs, half_groups, group, width)
    upstream = upstream.at[:, :, IMG_GROUP + 1, :].multiply(readout_scale[:, :, None])
    upstream = upstream.reshape(rows, width)
    per_layer = [None] * NL
    for which in reversed(range(NL)):
        upstream, parts = layer_backward(
            inputs_kept[which],
            middles[which],
            normeds[which],
            feed_normeds[which],
            totals[which],
            upstream,
            which,
        )
        per_layer[which] = parts
    stacked = [jnp.stack([per_layer[which][member] for which in range(NL)]) for member in range(9)]
    stacked = list(
        (
            lax.psum(stacked[0].astype(jnp.bfloat16), ("dp", "ctx")).astype(jnp.float32),
            lax.psum(stacked[1].astype(jnp.bfloat16), ("dp", "ctx")).astype(jnp.float32),
            lax.psum(stacked[2].astype(jnp.bfloat16), ("dp", "ctx")).astype(jnp.float32),
            lax.psum(stacked[3].astype(jnp.bfloat16), ("dp", "ctx")).astype(jnp.float32),
            lax.psum(stacked[4].astype(jnp.bfloat16), ("dp", "ctx")).astype(jnp.float32),
            lax.psum(stacked[5].astype(jnp.bfloat16), ("dp", "ctx")).astype(jnp.float32),
            lax.psum(stacked[6].astype(jnp.bfloat16), ("dp", "ctx")).astype(jnp.float32),
            lax.psum(stacked[7].astype(jnp.bfloat16), ("dp", "ctx")).astype(jnp.float32),
            lax.psum(stacked[8].astype(jnp.bfloat16), ("dp", "ctx")).astype(jnp.float32),
        )
    )
    mine = lax.dynamic_slice_in_dim(
        upstream.reshape(seqs, half_groups, group, width), column, width_dev, 3
    )
    picture_back = (
        mine[:, :, :IMG_GROUP]
        .reshape(seqs * half_groups * IMG_GROUP, width_dev)
        .astype(jnp.bfloat16)
    )
    words_back = mine[:, :, IMG_GROUP].reshape(seqs * half_groups, width_dev).astype(jnp.bfloat16)
    marker_back = jnp.sum(mine[:, :, IMG_GROUP + 1], axis=(0, 1))
    returned = lax.all_to_all(picture_back, "dp", split_axis=0, concat_axis=0, tiled=True)
    patch_weight_gradient = jnp.einsum(
        "rp,rn->pn", patches, returned, preferred_element_type=jnp.float32
    )
    patch_bias_gradient = jnp.sum(returned.astype(jnp.float32), axis=0)
    text_weight_gradient = jnp.einsum(
        "rl,rn->ln", text_flat, words_back, preferred_element_type=jnp.float32
    )
    text_bias_gradient = jnp.sum(words_back.astype(jnp.float32), axis=0)
    patch_terms = jnp.einsum(
        "rn,pn->rp", returned, patch_weight, preferred_element_type=jnp.float32
    )
    text_terms = jnp.einsum(
        "rn,ln->rl", words_back, text_weight, preferred_element_type=jnp.float32
    )
    patches_gradient, text_gradient = (
        lax.psum_scatter(
            patch_terms.astype(jnp.bfloat16), "tensor", scatter_dimension=1, tiled=True
        ).astype(jnp.float32),
        lax.psum_scatter(
            text_terms.astype(jnp.bfloat16), "tensor", scatter_dimension=1, tiled=True
        ).astype(jnp.float32),
    )
    stem = (
        lax.psum(patch_weight_gradient.astype(jnp.bfloat16), ("dp", "ctx")).astype(jnp.float32),
        lax.psum(patch_bias_gradient.astype(jnp.bfloat16), ("dp", "ctx")).astype(jnp.float32),
        lax.psum(text_weight_gradient.astype(jnp.bfloat16), ("dp", "ctx")).astype(jnp.float32),
        lax.psum(text_bias_gradient.astype(jnp.bfloat16), ("dp", "ctx")).astype(jnp.float32),
        lax.psum(marker_back.astype(jnp.bfloat16), ("dp", "ctx")).astype(jnp.float32),
    )
    text_gradient = text_gradient.reshape(seqs, half_groups, text_gradient.shape[1])
    return (
        activations,
        patches_gradient,
        text_gradient,
        stem[0],
        stem[1],
        stem[2],
        stem[3],
        stem[4],
        stacked[0],
        stacked[1],
        stacked[2],
        stacked[3],
        stacked[4],
        stacked[5],
        stacked[6],
        stacked[7],
        stacked[8],
    )


def solution(mesh):
    in_specs = (
        P(("dp", "ctx"), None),
        P("dp", "ctx", None),
        P(None, "tensor"),
        P("tensor"),
        P(None, "tensor"),
        P("tensor"),
        P("tensor"),
        P(),
        P(),
        P(None, None, None, "tensor"),
        P(None, "tensor", None),
        P(),
        P(),
        P(None, None, "tensor"),
        P(None, "tensor"),
        P(None, "tensor", None),
        P("dp", None),
        P("dp"),
        P(),
        P("dp", "ctx"),
        P("dp", "ctx", None),
    )
    out_specs = (
        P("dp", "ctx", "tensor"),
        P(("dp", "ctx"), "tensor"),
        P("dp", "ctx", "tensor"),
        P(None, "tensor"),
        P("tensor"),
        P(None, "tensor"),
        P("tensor"),
        P("tensor"),
        P(None, "tensor"),
        P(None, "tensor"),
        P(None, None, None, "tensor"),
        P(None, "tensor", None),
        P(None, "tensor"),
        P(None, "tensor"),
        P(None, None, "tensor"),
        P(None, "tensor"),
        P(None, "tensor", None),
    )
    return jax.shard_map(shards, mesh=mesh, in_specs=in_specs, out_specs=out_specs, check_vma=False)
```

profile of v0, /device:TPU:1, one launch (start us, length us, event | category | flops | bytes accessed | tf_op | source)
XLA Modules:
  0.0 875.9 jit_solution(269084299808295830)
XLA Ops:
  10.6 18.9 %all_to_all.21 = bf16[16,60,192]{2,1,0:T(8,128)(2,1)S(1)} all-to-all(bf16[16,60,192]{2,1,0:T(8,128)(2,1)S(1)} %all_to_all.14), channel_id=1, replica_groups=mesh['dp'=16,'ctx'=2,'tensor'=4] {'dp'}, dimensions={0} | all-to-all | bytes 737280 | tf_op jit(solution)/shard_map/all_to_all | solution.py:232
  30.9 9.4 %all-gather = bf16[4,192,32]{1,2,0:T(8,128)(2,1)S(1)} all-gather(bf16[1,192,32]{1,2,0:T(8,128)(2,1)S(1)} %fusion.86), channel_id=1, replica_groups=mesh['dp'=16,'ctx'=2,'tensor'=4] {'tensor'}, dimensions={0}, use_global_device_ids=true | all-gather | bytes 61440 | tf_op jit(solution)/shard_map/all_gather | solution.py:235
  42.0 8.6 all-reduce
  51.9 2.8 fusion.142
  56.3 2.6 copy.119
  58.9 2.3 reshape.442
  70.3 7.1 all_gather.29
  80.4 2.6 all_gather.28
  83.2 3.2 fusion.145
  89.0 2.2 fusion.63
  93.8 45.5 %all-reduce.13.cloned.1.call-done = bf16[1024,768]{1,0:T(8,128)(2,1)} async-done(((bf16[1024,768]{1,0:T(8,128)(2,1)}), bf16[1024,768]{1,0:T(8,128)(2,1)}) %all-reduce.13.cloned.1.call-update) | async-done | bytes 1572880 | tf_op jit(solution)/shard_map/psum | solution.py:268
  139.2 2.3 fusion.48
  147.3 3.2 convolution_convert_fusion.5
  150.7 50.6 %all-reduce.15.cloned.1.call-done = bf16[1024,768]{1,0:T(8,128)(2,1)} async-done(((bf16[1024,768]{1,0:T(8,128)(2,1)}), bf16[1024,768]{1,0:T(8,128)(2,1)}) %all-reduce.15.cloned.1.call-update) | async-done | bytes 1572880 | tf_op jit(solution)/shard_map/psum | solution.py:277
  201.2 2.8 fusion.141
  212.8 3.0 all_gather.31
  218.8 3.0 all_gather.30
  222.0 3.2 fusion.146
  227.8 2.2 fusion.64
  236.0 2.3 scatter-mul.4
  238.3 5.1 bitcast_convert_fusion.2
  243.4 39.0 %all-reduce.17.cloned.1.call-done = bf16[1024,768]{1,0:T(8,128)(2,1)} async-done(((bf16[1024,768]{1,0:T(8,128)(2,1)}), bf16[1024,768]{1,0:T(8,128)(2,1)}) %all-reduce.17.cloned.1.call-update) | async-done | bytes 1572880 | tf_op jit(solution)/shard_map/psum | solution.py:268
  282.4 2.7 fusion.140
  291.4 4.3 fusion.147
  296.9 2.6 convolution_convert_fusion.2
  299.7 50.4 %all-reduce.19.cloned.1.call-done = bf16[1024,768]{1,0:T(8,128)(2,1)} async-done(((bf16[1024,768]{1,0:T(8,128)(2,1)}), bf16[1024,768]{1,0:T(8,128)(2,1)}) %all-reduce.19.cloned.1.call-update) | async-done | bytes 1572880 | tf_op jit(solution)/shard_map/psum | solution.py:129
  350.1 3.5 convert_reduce_fusion.3
  362.4 5.0 convolution_convert_fusion.12
  367.5 5.2 multiply_reduce_fusion.1
  372.7 3.6 multiply_convert_fusion.1
  378.3 3.3 fusion.62
  390.5 3.5 reduce-scatter.9.cloned.1.call-done
  401.6 4.1 bitcast_convert_fusion.1
  406.2 50.9 %all-reduce.21.cloned.1.call-done = bf16[1024,768]{1,0:T(8,128)(2,1)} async-done(((bf16[1024,768]{1,0:T(8,128)(2,1)}), bf16[1024,768]{1,0:T(8,128)(2,1)}) %all-reduce.21.cloned.1.call-update) | async-done | bytes 1572880 | tf_op jit(solution)/shard_map/psum | solution.py:203
  457.0 3.5 convert_reduce_fusion.2
  460.8 2.4 fusion.31
  465.9 4.3 fusion.148
  471.3 2.6 convolution_convert_fusion.1
  474.0 50.6 %all-reduce.23.cloned.1.call-done = bf16[1024,768]{1,0:T(8,128)(2,1)} async-done(((bf16[1024,768]{1,0:T(8,128)(2,1)}), bf16[1024,768]{1,0:T(8,128)(2,1)}) %all-reduce.23.cloned.1.call-update) | async-done | bytes 1572880 | tf_op jit(solution)/shard_map/psum | solution.py:129
  524.6 4.1 convert_reduce_fusion.1
  528.7 3.1 fusion.32
  538.8 4.9 convolution_convert_fusion.11
  543.8 5.2 multiply_reduce_fusion
  549.1 3.6 multiply_convert_fusion
  554.9 5.6 convolution_convert_fusion.3
  578.1 4.1 bitcast_convert_fusion
  582.4 4.3 fusion.59
  587.9 4.2 fusion.60
  592.5 2.5 fusion.51
  595.0 3.0 fusion.53
  599.8 2.5 fusion.152
  602.3 56.7 %all-reduce.27.cloned.1.call-done = (bf16[1024,768]{1,0:T(8,128)(2,1)}, bf16[1024,768]{1,0:T(8,128)(2,1)}) async-done(((bf16[1024,768]{1,0:T(8,128)(2,1)}, bf16[1024,768]{1,0:T(8,128)(2,1)}), (bf16[1024,768]{1,0:T(8,128)(2,1)}, bf16[1024,768]{1,0:T(8,128)(2,1)})) %all-reduce.27.cloned.1.call-update) | async-done | bytes 3145744 | tf_op jit(solution)/shard_map/psum | solution.py:277
  659.1 3.4 convert_reduce_fusion
  662.5 3.9 fusion.33
  670.0 6.7 all-to-all-start.1
  680.4 6.8 all-to-all-done.1
  687.4 2.7 convolution_convert_fusion
  690.5 3.5 fusion.50
  712.1 2.3 fusion.87
  718.6 66.6 %all-reduce.1 = (bf16[192]{0:T(256)(128)(2,1)S(1)}, bf16[192]{0:T(256)(128)(2,1)S(1)}, bf16[192]{0:T(256)(128)(2,1)S(1)}, bf16[2,192]{1,0:T(2,128)(2,1)S(1)}, bf...) all-reduce(bf16[192]{0:T(256)(128)(2,1)S(1)} %reduce_sum.344, ...), channel_id=1, replica_groups=mesh['dp'=16,'ctx'=2,'tensor'=4] {'dp','ctx'}, use_global_device_ids=true, to_apply=%region_39.40 | all-reduce | flops 3648 | bytes 14592 | tf_op jit(solution)/shard_map/psum | solution.py:363
  791.7 63.9 %all-reduce.25.cloned.1.call-done = (bf16[768,192]{0,1:T(8,128)(2,1)}, bf16[768,192]{0,1:T(8,128)(2,1)}, bf16[2,768,3,192]{1,3,2,0:T(8,128)(2,1)}, bf16[2,192,76...) async-done(((bf16[768,192]{0,1:T(8,128)(2,1)}, bf16[768,192]{0,1:T(8,128)(2,1)}, bf16[2,768,3,192]{1,3,2,0:T(8,128)(2,1)}, ...) | async-done | bytes 7667728 | tf_op jit(solution)/shard_map/psum | solution.py:362
  859.4 2.3 convert_element_type.443
  863.8 2.5 convert_element_type.446
  866.3 2.5 convert_element_type.451
  (397 shorter events, 164.3 us)
Async XLA Ops:
  7.2 49.1 %all-gather.3.cloned.1.call-start = ((), (), s32[]{:S(2)}) async-start(), calls=%async_computation.8 | async-start | bytes 1966080 | tf_op jit(solution)/shard_map/all_gather | solution.py:234
  10.2 20.6 %copy-start.50 = (bf16[768,192]{0,1:T(8,128)(2,1)S(1)}, bf16[768,192]{0,1:T(8,128)(2,1)}, u32[]{:S(2)}) copy-start(bf16[768,192]{0,1:T(8,128)(2,1)} %param.27) | copy-start | bytes 884740
  10.2 20.6 %copy-start.57 = (bf16[4,8,768]{2,1,0:T(8,128)(2,1)S(1)}, bf16[4,8,768]{2,1,0:T(8,128)(2,1)}, u32[]{:S(2)}) copy-start(bf16[4,8,768]{2,1,0:T(8,128)(2,1)} %param.24) | copy-start | bytes 147460
  10.2 20.5 %copy-start.74 = (f32[192]{0:T(256)S(1)}, f32[192]{0:T(256)}, u32[]{:S(2)}) copy-start(f32[192]{0:T(256)} %param.28) | copy-start | bytes 2308
  10.2 30.3 %copy-start.84 = (u32[128]{0:T(128)S(1)}, u32[128]{0:T(128)}, u32[]{:S(2)}) copy-start(u32[128]{0:T(128)} %constant.112) | copy-start | bytes 1540
  10.2 31.6 %copy-start.81 = (bf16[192]{0:T(256)(128)(2,1)S(1)}, bf16[192]{0:T(256)(128)(2,1)}, u32[]{:S(2)}) copy-start(bf16[192]{0:T(256)(128)(2,1)} %param.29) | copy-start | bytes 1156
  10.2 40.4 %copy-start.65 = (s32[4,512]{1,0:T(4,128)S(1)}, s32[4,512]{1,0:T(4,128)}, u32[]{:S(2)}) copy-start(s32[4,512]{1,0:T(4,128)} %param.39) | copy-start | bytes 24580
  10.2 40.4 %copy-start.66 = (f32[2,768]{1,0:T(2,128)S(1)}, f32[2,768]{1,0:T(2,128)}, u32[]{:S(2)}) copy-start(f32[2,768]{1,0:T(2,128)} %param.31) | copy-start | bytes 18436
  10.2 40.4 %copy-start.67 = (f32[2,768]{1,0:T(2,128)S(1)}, f32[2,768]{1,0:T(2,128)}, u32[]{:S(2)}) copy-start(f32[2,768]{1,0:T(2,128)} %param.30) | copy-start | bytes 18436
  30.6 108.6 %all-reduce.13.cloned.1.call-start = ((), (), s32[]{:S(2)}) async-start(), calls=%async_computation.9 | async-start | bytes 3145728 | tf_op jit(solution)/shard_map/psum | solution.py:268
  50.7 12.0 %copy-start.61 = (f32[768]{0:T(1024)}, f32[768]{0:T(1024)S(1)}, u32[]{:S(2)}) copy-start(f32[768]{0:T(1024)S(1)} %get-tuple-element.170) | copy-start | bytes 9220
  50.7 12.0 %copy-start.63 = (f32[768]{0:T(1024)}, f32[768]{0:T(1024)S(1)}, u32[]{:S(2)}) copy-start(f32[768]{0:T(1024)S(1)} %get-tuple-element.122) | copy-start | bytes 9220
  83.2 4.7 copy-start.27
  93.4 107.9 %all-reduce.15.cloned.1.call-start = ((), (), s32[]{:S(2)}) async-start(), calls=%async_computation.10 | async-start | bytes 3145728 | tf_op jit(solution)/shard_map/psum | solution.py:277
  144.3 3.1 copy-start.78
  150.6 131.7 %all-reduce.17.cloned.1.call-start = ((), (), s32[]{:S(2)}) async-start(), calls=%async_computation.11 | async-start | bytes 3145728 | tf_op jit(solution)/shard_map/psum | solution.py:268
  222.0 4.7 copy-start.28
  232.2 118.0 %all-reduce.19.cloned.1.call-start = ((), (), s32[]{:S(2)}) async-start(), calls=%async_computation.12 | async-start | bytes 3145728 | tf_op jit(solution)/shard_map/psum | solution.py:129
  287.9 3.5 copy-start.79
  289.3 6.4 copy-start.88
  299.5 87.0 %reduce-scatter.11.cloned.1.call-start = ((), (), s32[]{:S(2)}) async-start(), calls=%async_computation.14 | async-start | bytes 1179648 | tf_op jit(solution)/shard_map/reduce_scatter | solution.py:179
  350.1 3.6 copy-start.6
  350.1 3.8 copy-start.20
  355.8 3.2 copy-start.38
  367.4 26.6 %reduce-scatter.9.cloned.1.call-start = ((), (), s32[]{:S(2)}) async-start(), calls=%async_computation.13 | async-start | bytes 1179648 | tf_op jit(solution)/shard_map/reduce_scatter | solution.py:173
  372.7 3.6 copy-start.32
  378.3 78.7 %all-reduce.21.cloned.1.call-start = ((), (), s32[]{:S(2)}) async-start(), calls=%async_computation.15 | async-start | bytes 3145728 | tf_op jit(solution)/shard_map/psum | solution.py:203
  405.7 118.8 %all-reduce.23.cloned.1.call-start = ((), (), s32[]{:S(2)}) async-start(), calls=%async_computation.16 | async-start | bytes 3145728 | tf_op jit(solution)/shard_map/psum | solution.py:129
  457.0 3.5 copy-start.4
  457.0 3.8 copy-start.21
  460.5 2.7 copy-start.10
  465.8 4.3 copy-start.24
  465.8 5.5 copy-start.77
  473.9 92.5 %reduce-scatter.15.cloned.1.call-start = ((), (), s32[]{:S(2)}) async-start(), calls=%async_computation.18 | async-start | bytes 1179648 | tf_op jit(solution)/shard_map/reduce_scatter | solution.py:179
  524.6 4.1 copy-start.8
  524.6 4.2 copy-start.22
  528.7 3.1 copy-start.25
  531.8 3.6 copy-start.39
  543.8 26.7 %reduce-scatter.13.cloned.1.call-start = ((), (), s32[]{:S(2)}) async-start(), calls=%async_computation.17 | async-start | bytes 1179648 | tf_op jit(solution)/shard_map/reduce_scatter | solution.py:173
  549.1 3.6 copy-start.31
  554.7 104.4 %all-reduce.27.cloned.1.call-start = ((), (), s32[]{:S(2)}) async-start(), calls=%async_computation.22 | async-start | bytes 6291456 | tf_op jit(solution)/shard_map/psum | solution.py:277
  554.9 5.7 copy-start.16
  554.9 5.6 copy-start.30
  582.4 5.5 copy-start.29
  587.9 4.5 copy-start.47
  587.9 4.5 copy-start.91
  595.0 3.0 copy-start.11
  599.8 59.2 %copy-start.62 = (f32[768]{0:T(1024)S(1)}, f32[768]{0:T(1024)}, u32[]{:S(2)}) copy-start(f32[768]{0:T(1024)} %copy-done.61) | copy-start | bytes 9220
  602.3 60.1 %copy-start.64 = (f32[768]{0:T(1024)S(1)}, f32[768]{0:T(1024)}, u32[]{:S(2)}) copy-start(f32[768]{0:T(1024)} %copy-done.63) | copy-start | bytes 9220
  659.1 3.4 copy-start.23
  662.4 3.9 copy-start.13
  668.7 10.6 %copy-start.51 = (bf16[768,192]{0,1:T(8,128)(2,1)S(1)}, bf16[768,192]{0,1:T(8,128)(2,1)}, u32[]{:S(2)}) copy-start(bf16[768,192]{0,1:T(8,128)(2,1)} %param.27) | copy-start | bytes 884740
  670.0 17.2 %all-to-all-start.1 = ((bf16[16,60,192]{2,1,0:T(8,128)(2,1)}), bf16[16,60,192]{2,1,0:T(8,128)(2,1)S(1)}, u32[]{:S(2)}, u32[]{:S(2)}) async-start(bf16[16,60,192]{2,1,0:T(8,128)(2,1)} %convert_element_type.419), calls=%async_computation.5 | async-start | bytes 1048576 | tf_op jit(solution)/shard_map/all_to_all | solution.py:338
  676.7 40.2 %reduce-scatter.19.cloned.1.call-start = ((), (), s32[]{:S(2)}) async-start(), calls=%async_computation.20 | async-start | bytes 245760
  680.4 109.4 %reduce-scatter.17.cloned.1.call-start = ((), (), s32[]{:S(2)}) async-start(), calls=%async_computation.19 | async-start | bytes 1966080 | tf_op jit(solution)/shard_map/reduce_scatter | solution.py:354
  690.2 165.4 %all-reduce.25.cloned.1.call-start = ((), (), s32[]{:S(2)}) async-start(), calls=%async_computation.21 | async-start | bytes 15335424 | tf_op jit(solution)/shard_map/psum | solution.py:362
  690.5 3.5 copy-start.53
  690.5 5.1 copy-start.87
  694.0 2.8 copy-start.26
  698.8 2.7 copy-start.14
  698.8 2.8 copy-start.41
  698.8 3.3 copy-start.54
  855.6 6.1 copy-start.40
  859.4 4.4 copy-start.35
  (45 other events, 89.1 us)
Sparse Core Ops, SparseCore 0:
  30.8 25.4 all-gather.2
  93.5 45.6 all-reduce.12
  150.7 50.4 all-reduce.14
  232.3 50.0 all-reduce.16
  299.6 50.4 all-reduce.18
  367.6 11.6 reduce-scatter.10
  381.7 12.2 reduce-scatter.8
  405.8 51.1 all-reduce.20
  474.0 50.4 all-reduce.22
  543.9 11.5 reduce-scatter.14
  558.0 12.2 reduce-scatter.12
  582.4 76.6 all-reduce.26
  680.5 18.6 reduce-scatter.18
  701.6 26.6 reduce-scatter.16
  734.2 121.3 all-reduce.24
where the time goes:
time: 886 us; the launch traced here: 876 us
  waiting for transfers between devices  420 us (47%)
  blocking collectives  119 us (13%)
  matrix products  113 us (13%)
  local copies, waits for them, and re-layouts  103 us (12%)
  other arithmetic  96.3 us (11%)
  between operations  16.4 us (2%)
    psum x2, waiting for transfers between devices, shards(): lax.psum(layer_feed_terms.astype(jnp.bfloat16), 'tensor')  107 us
    psum x2, waiting for transfers between devices, layer_backward(): lax.psum(feed_terms.astype(jnp.bfloat16), 'tensor').astype(jnp.float32)  101 us
    psum x2, waiting for transfers between devices, shards(): lax.psum(layer_mix_terms.astype(jnp.bfloat16), 'tensor').astype(jnp.float32)  84.5 us
    psum x1, blocking collectives, shards(): lax.psum(patch_bias_gradient.astype(jnp.bfloat16), ('dp', 'ctx'))  66.6 us
    psum x1, waiting for transfers between devices, shards(): lax.psum(patch_weight_gradient.astype(jnp.bfloat16), ('dp', 'ctx'))  63.9 us
    psum x1, waiting for transfers between devices, layer_backward(): lax.psum(mix_terms.astype(jnp.bfloat16), 'tensor').astype(jnp.float32)  50.9 us
    unnamed x202, local copies, waits for them, and re-layouts  35.2 us
    reduce_sum x8, other arithmetic, normalize(): return centred * lax.rsqrt(spread + EPS) * gain_row + shift_row  25.8 us
  transfers between devices with their start and end apart: 16, of which 11 were waited for; matrix products, arithmetic and copies ran while one was open for 14% of the time, Pallas kernels for 0%

commit v1 on v0

v1 whole, which is shorter than its diff:
```python
import jax
import jax.numpy as jnp
from jax import lax
from jax.experimental import pallas as pl
from jax.experimental.pallas import tpu as pltpu
from jax.sharding import PartitionSpec as P

HEAD_DIM = 64
HEADS = 12
NL = 2
L = 512
HALF = 256
D = 768
DEV = 192
IMG_GROUP = 30
EPS = 1e-06
MASKED = -1e30
MESH = pl.DeviceIdType.MESH
BF = jnp.bfloat16
F32 = jnp.float32

STEM = 384
LAYER = 2304
ROWS = STEM + NL * LAYER

GATHER_UNITS = [
    (0, 128, 512, 512),
    (1152, 256, 512, 0),
    (1920, 256, 0, 512),
    (2688, 256, 512, 0),
    (3456, 256, 0, 512),
    (4224, 256, 512, 0),
]

GRAD_ROWS = NL * LAYER + 512


def place():
    d = lax.axis_index("dp")
    c = lax.axis_index("ctx")
    t = lax.axis_index("tensor")
    return d // 4, d % 4, c, t


def peer(axis, r):
    z, y, c, t = place()
    if axis == "x":
        return (z * 4 + y, c, (t + r) % 4)
    if axis == "y":
        return (z * 4 + (y + r) % 4, c, t)
    return (((z + r) % 4) * 4 + y, c, t)


def sibling():
    z, y, c, t = place()
    return (z * 4 + y, 1 - c, t)


def greet(stem):
    z, y, c, t = place()
    bar = pltpu.get_barrier_semaphore()
    for axis in "xyz":
        for r in (1, 2, 3):
            pl.semaphore_signal(bar, inc=1, device_id=peer(axis, r), device_id_type=MESH)
    pl.semaphore_signal(bar, inc=1, device_id=sibling(), device_id_type=MESH)
    if stem is None:
        pl.semaphore_wait(bar, 10)
        return

    def hello(i, carry):
        if stem == "in":
            other = (t * 4 + i // 4, c, i % 4)
        else:
            other = (i, c, z)
        me = (z * 4 + y == other[0]) & (t == other[2])

        @pl.when(jnp.logical_not(me))
        def _():
            pl.semaphore_signal(bar, inc=1, device_id=other, device_id_type=MESH)

        return carry

    lax.fori_loop(0, 16, hello, 0)
    own = t == z

    @pl.when(own)
    def _():
        pl.semaphore_wait(bar, 25)

    @pl.when(jnp.logical_not(own))
    def _():
        pl.semaphore_wait(bar, 26)


def remote(src, dst, send, recv, device):
    return pltpu.make_async_remote_copy(
        src_ref=src, dst_ref=dst, send_sem=send, recv_sem=recv, device_id=device, device_id_type=MESH
    )


class Gather:
    def __init__(self, buf, send, recv):
        self.buf, self.send, self.recv = buf, send, recv

    def x_copies(self, unit, sem, row, rows):
        return [
            remote(
                self.buf.at[0, pl.ds(row, rows)],
                self.buf.at[r, pl.ds(row, rows)],
                self.send.at[unit, sem + r - 1],
                self.recv.at[unit, sem + r - 1],
                peer("x", -r),
            )
            for r in (1, 2, 3)
        ]

    def plane_copies(self, unit, sem, device, row, rows):
        region = self.buf.at[pl.ds(1, 3), pl.ds(row, rows)]
        return remote(region, region, self.send.at[unit, sem], self.recv.at[unit, sem], device)

    def stage(self, unit, which):
        first, nx, nyz, nzy = GATHER_UNITS[unit]
        z, y, c, t = place()
        m = lambda v: pl.multiple_of(v, 16)
        out = []
        if which == 0:
            return self.x_copies(unit, 0, m(first + c * (nx // 2)), nx // 2)
        if which == 4:
            parts = [(first, nx), (first + nx, nyz), (first + nx + nyz, nzy)]
            for k, (row, rows) in enumerate(parts):
                if rows:
                    out.append(self.plane_copies(unit, 21 + k, sibling(), m(row + c * (rows // 2)), rows // 2))
            return out
        for sem, slow, fast, row, rows in (
            (3, ("z", z), ("y", y), first + nx, nyz),
            (12, ("y", y), ("z", z), first + nx + nyz, nzy),
        ):
            if not rows:
                continue
            row = row + c * 256 + slow[1] * 64
            if which == 1:
                out += self.x_copies(unit, sem, m(row + fast[1] * 16), 16)
            for r in (1, 2, 3):
                if which == 2:
                    out.append(self.plane_copies(unit, sem + 2 + r, peer(fast[0], -r), m(row + fast[1] * 16), 16))
                if which == 3:
                    out.append(self.plane_copies(unit, sem + 5 + r, peer(slow[0], -r), m(row), 64))
        return out

    def start(self, unit, which):
        for copy in self.stage(unit, which):
            copy.start()

    def arrived(self, unit, which):
        for copy in self.stage(unit, which):
            copy.wait_recv()

    def finish(self, unit):
        for which in range(5):
            for copy in self.stage(unit, which):
                copy.wait_send()


def scatter_patches(stage, out, send, recv, own, mode):
    z, y, c, t = place()
    rows = pl.ds(pl.multiple_of(t * 16, 16), 16)

    def each(i, carry):
        to_me = (z * 4 + y == i) & (t == z)
        local = pltpu.make_async_copy(stage.at[i], out.at[y, rows], own)
        away = remote(stage.at[i], out.at[y, rows], send.at[i], recv.at[y * 4 + t], (i, c, z))

        @pl.when(to_me)
        def _():
            local.start() if mode == "start" else local.wait()

        @pl.when(jnp.logical_not(to_me))
        def _():
            away.start() if mode == "start" else away.wait_send()

        return carry

    def arrive(i, carry):
        from_me = (t == z) & (i // 4 == y) & (i % 4 == t)
        there = pl.ds(pl.multiple_of((i % 4) * 16, 16), 16)

        @pl.when(jnp.logical_not(from_me))
        def _():
            region = out.at[i // 4, there]
            remote(region, region, send.at[i], recv.at[i], (i, c, z)).wait_recv()

        return carry

    lax.fori_loop(0, 16, each, 0)
    if mode == "wait":
        lax.fori_loop(0, 16, arrive, 0)


def dot_nt(a, b):
    return lax.dot_general(a, b, (((1,), (1,)), ((), ())), preferred_element_type=F32)


def dot_tn(a, b):
    return lax.dot_general(a, b, (((0,), (0,)), ((), ())), preferred_element_type=F32)


def dot_nn(a, b):
    return jnp.dot(a, b, preferred_element_type=F32)


def row_blocks(size, body):
    def step(i, carry):
        body(pl.ds(pl.multiple_of(i * size, size), size))
        return carry

    lax.fori_loop(0, HALF // size, step, 0)


def norm_rows(src, gain, shift, dst):
    def body(rows):
        x = src[rows]
        mean = jnp.mean(x, axis=-1, keepdims=True)
        centred = x - mean
        spread = jnp.mean(centred * centred, axis=-1, keepdims=True)
        dst[rows] = (centred * lax.rsqrt(spread + EPS) * gain + shift).astype(BF)

    row_blocks(64, body)


GELU_A = 0.7978845608028654
GELU_B = 0.044715


def gather_kernel(
    patch_w,
    text_w,
    in_w,
    out_w,
    up_w,
    down_w,
    vectors,
    gains,
    stamps_q,
    stamps_k,
    patches,
    words,
    w_out,
    patch_out,
    vec_out,
    xs_out,
    mid_out,
    nrm_out,
    fn_out,
    tri_out,
    kvo_out,
    mix_out,
    lse_out,
    pre_out,
    act_out,
    buf,
    vec,
    gain,
    stamp_q,
    stamp_k,
    pstage,
    prow,
    word,
    xs,
    mid,
    nrm,
    fn,
    tri,
    kvo,
    mix,
    lse,
    pre,
    act,
    bias,
    hid,
    local,
    send,
    recv,
    psend,
    precv,
    own,
    vsend,
    vrecv,
    ksend,
    krecv,
    saved,
):
    z, y, c, t = place()
    early = [
        pltpu.make_async_copy(patches.at[:, pl.ds(pl.multiple_of(t * 16, 16), 16)], pstage, local.at[0]),
        pltpu.make_async_copy(vectors, vec.at[0], local.at[1]),
    ]
    sources = [(patch_w, 0, 192), (text_w, 192, 192)]
    for which in range(NL):
        base = STEM + which * LAYER
        sources += [
            (in_w.at[which], base, 576),
            (out_w.at[which], base + 576, 192),
            (up_w.at[which], base + 768, 768),
            (down_w.at[which], base + 1536, 768),
        ]
    loads = [
        pltpu.make_async_copy(ref, buf.at[0, pl.ds(row, rows)], local.at[2 + k])
        for k, (ref, row, rows) in enumerate(sources)
    ]
    late = [
        pltpu.make_async_copy(words, word, local.at[12]),
        pltpu.make_async_copy(gains, gain, local.at[13]),
        pltpu.make_async_copy(stamps_q, stamp_q, local.at[14]),
        pltpu.make_async_copy(stamps_k, stamp_k, local.at[15]),
    ]
    for copy in early + loads + late:
        copy.start()
    greet("in")
    early[0].wait()
    scatter_patches(pstage, prow, psend, precv, own, "start")
    early[1].wait()
    vec_copies = [
        remote(vec.at[0], vec.at[r], vsend.at[r - 1], vrecv.at[r - 1], peer("x", -r)) for r in (1, 2, 3)
    ]
    for copy in vec_copies:
        copy.start()
    units = [[0, 1, 2, 3], [4], [5], [6, 7], [8], [9]]
    g = Gather(buf, send, recv)
    for unit, members in enumerate(units):
        for k in members:
            loads[k].wait()
        g.start(unit, 1)
    for unit in range(6):
        g.start(unit, 0)
    for unit in range(6):
        g.arrived(unit, 1)
        g.start(unit, 2)
    for unit in range(6):
        g.arrived(unit, 2)
        g.start(unit, 3)
    for copy in late:
        copy.wait()

    lse[...] = jnp.zeros_like(lse)

    def see(i, carry):
        rows = pl.ds(pl.multiple_of(i * 64, 64), 64)
        bias[rows] = jnp.where(stamp_k[rows, 0:1] <= stamp_q[0:1, :], 0.0, MASKED)
        return carry

    lax.fori_loop(0, 8, see, 0)

    scatter_patches(pstage, prow, psend, precv, own, "wait")
    for copy in vec_copies:
        copy.wait()

    saves = []

    def save(k, src, dst):
        copy = pltpu.make_async_copy(src, dst, saved.at[k])
        copy.start()
        saves.append(copy)

    def ready(unit):
        g.arrived(unit, 0)
        g.arrived(unit, 3)
        g.start(unit, 4)
        g.arrived(unit, 4)

    ready(0)
    place_in = lax.broadcasted_iota(jnp.int32, (HALF, 1), 0) % (IMG_GROUP + 2)
    parts = []
    for a in range(4):
        s = (a - t) % 4
        picture = dot_nt(prow[...].reshape(HALF, D), buf[s, 0:192]) + vec[s, 2:3, 0:192]
        language = dot_nt(word[...], buf[s, 192:384]) + vec[s, 3:4, 0:192]
        mark = vec[s, 4:5, 0:192]
        part = jnp.where(place_in < IMG_GROUP, picture, jnp.where(place_in == IMG_GROUP, language, mark))
        parts.append(part.astype(BF).astype(F32))
    xs[0] = jnp.concatenate(parts, axis=1)
    save(0, prow, patch_out)
    save(1, vec, vec_out)

    for which in range(NL):
        base = STEM + which * LAYER
        if which:
            ready(3)
        norm_rows(xs.at[which], gain[which : which + 1], gain[2 + which : 3 + which], nrm.at[which])

        def project(s, carry):
            triple = dot_nt(buf[s, base : base + 576], nrm[which])
            tri[which, s] = triple.astype(BF)
            remote(
                tri.at[which, s, pl.ds(192, 384)],
                kvo.at[which, s],
                ksend.at[which, s],
                krecv.at[which, s],
                sibling(),
            ).start()
            return carry

        lax.fori_loop(0, 4, project, 0)
        mid[which] = xs[which]

        def attend(s, carry):
            remote(
                tri.at[which, s, pl.ds(192, 384)],
                kvo.at[which, s],
                ksend.at[which, s],
                krecv.at[which, s],
                sibling(),
            ).wait_recv()
            for h in range(3):
                at = 64 * h
                q = tri[which, s, at : at + 64] * jnp.asarray(HEAD_DIM**-0.5, BF)
                one = dot_tn(tri[which, s, 192 + at : 256 + at], q) + bias[0:256]
                two = dot_tn(kvo[which, s, at : at + 64], q) + bias[256:512]
                top = jnp.maximum(jnp.max(one, axis=0, keepdims=True), jnp.max(two, axis=0, keepdims=True))
                one = jnp.exp(one - top)
                two = jnp.exp(two - top)
                total = jnp.sum(one, axis=0, keepdims=True) + jnp.sum(two, axis=0, keepdims=True)
                lse[which, s, h : h + 1] = top + jnp.log(total)
                scale = 1.0 / total
                one = (one * scale).astype(BF)
                two = (two * scale).astype(BF)
                mixed = dot_nn(tri[which, s, 384 + at : 448 + at], one)
                mixed = mixed + dot_nn(kvo[which, s, 192 + at : 256 + at], two)
                mix[which, s, at : at + 64] = mixed.astype(BF)
            mid[which] += dot_tn(mix[which, s], buf[s, base + 576 : base + 768])
            return carry

        lax.fori_loop(0, 4, attend, 0)
        norm_rows(mid.at[which], gain[4 + which : 5 + which], gain[6 + which : 7 + which], fn.at[which])
        ready(1 + 3 * which)

        def lift(s, carry):
            pre[which, s] = dot_nn(fn[which], buf[s, base + 768 : base + 1536]) + vec[s, which : which + 1]
            return carry

        lax.fori_loop(0, 4, lift, 0)
        xs[which + 1] = mid[which]
        ready(2 + 3 * which)

        def lower(s, carry):
            def body(rows):
                x = pre[which, s, rows]
                hid[rows] = (0.5 * x * (1.0 + jnp.tanh(GELU_A * (x + GELU_B * x * x * x)))).astype(BF)

            row_blocks(64, body)
            xs[which + 1] += dot_nn(hid[...], buf[s, base + 1536 : base + 2304])
            return carry

        lax.fori_loop(0, 4, lower, 0)
        save(2 + which, pre.at[which], pre_out.at[which])

    save(4, buf, w_out)
    save(5, xs.at[pl.ds(0, 2)], xs_out)
    save(6, mid, mid_out)
    save(7, nrm, nrm_out)
    save(8, fn, fn_out)
    save(9, tri, tri_out)
    save(10, kvo, kvo_out)
    save(11, mix, mix_out)
    save(12, lse, lse_out)
    flipped = xs[2].astype(BF).T
    for a in range(4):
        act[a] = flipped[192 * a : 192 * a + 192]
    save(13, act, act_out)
    for which in range(NL):
        for s in range(4):
            remote(
                tri.at[which, s, pl.ds(192, 384)],
                kvo.at[which, s],
                ksend.at[which, s],
                krecv.at[which, s],
                sibling(),
            ).wait_send()
    for unit in range(6):
        g.finish(unit)
    for copy in saves:
        copy.wait()


def forward_call(*args):
    any_ = pl.BlockSpec(memory_space=pl.ANY)
    sds = jax.ShapeDtypeStruct
    shapes = [
        ((4, ROWS, D), BF),
        ((4, 64, D), BF),
        ((4, 8, D), F32),
        ((2, HALF, D), F32),
        ((2, HALF, D), F32),
        ((2, HALF, D), BF),
        ((2, HALF, D), BF),
        ((2, 4, 576, HALF), BF),
        ((2, 4, 384, HALF), BF),
        ((2, 4, 192, HALF), BF),
        ((2, 4, 8, HALF), F32),
        ((2, 4, HALF, D), F32),
        ((4, 192, HALF), BF),
    ]
    dma = pltpu.SemaphoreType.DMA
    return pl.pallas_call(
        gather_kernel,
        out_shape=tuple(sds(s, d) for s, d in shapes),
        in_specs=[any_] * 12,
        out_specs=(any_,) * len(shapes),
        scratch_shapes=[
            pltpu.VMEM((4, ROWS, D), BF),
            pltpu.VMEM((4, 8, D), F32),
            pltpu.VMEM((8, D), F32),
            pltpu.VMEM((8, HALF), jnp.int32),
            pltpu.VMEM((L, 128), jnp.int32),
            pltpu.VMEM((16, 16, D), BF),
            pltpu.VMEM((4, 64, D), BF),
            pltpu.VMEM((HALF, D), BF),
            pltpu.VMEM((3, HALF, D), F32),
            pltpu.VMEM((2, HALF, D), F32),
            pltpu.VMEM((2, HALF, D), BF),
            pltpu.VMEM((2, HALF, D), BF),
            pltpu.VMEM((2, 4, 576, HALF), BF),
            pltpu.VMEM((2, 4, 384, HALF), BF),
            pltpu.VMEM((2, 4, 192, HALF), BF),
            pltpu.VMEM((2, 4, 8, HALF), F32),
            pltpu.VMEM((2, 4, HALF, D), F32),
            pltpu.VMEM((4, 192, HALF), BF),
            pltpu.VMEM((L, HALF), F32),
            pltpu.VMEM((HALF, D), BF),
            dma((16,)),
            dma((6, 24)),
            dma((6, 24)),
            dma((16,)),
            dma((16,)),
            dma,
            dma((3,)),
            dma((3,)),
            dma((2, 4)),
            dma((2, 4)),
            dma((14,)),
        ],
        compiler_params=pltpu.CompilerParams(
            collective_id=0, has_side_effects=True, vmem_limit_bytes=63 * 2**20
        ),
    )(*args)


def prepare(
    patches,
    text_features,
    patch_weight,
    patch_bias,
    text_weight,
    text_bias,
    readout,
    mix_gain,
    mix_shift,
    heads_in_weight,
    heads_out_weight,
    feed_gain,
    feed_shift,
    up_weight,
    up_bias,
    down_weight,
    timesteps,
):
    t = lax.axis_index("tensor")
    c = lax.axis_index("ctx")
    wide = lambda v: jnp.pad(v.astype(F32), (0, D - DEV))[None]
    vectors = jnp.concatenate(
        [up_bias, wide(patch_bias), wide(text_bias), wide(readout), jnp.zeros((3, D), F32)], axis=0
    )
    gains = jnp.concatenate([mix_gain, mix_shift, feed_gain, feed_shift], axis=0)
    stamps = lax.dynamic_slice_in_dim(timesteps, t, 1, 0).reshape(2, HALF)
    mine = lax.dynamic_slice_in_dim(stamps, c, 1, 0)
    other = lax.dynamic_slice_in_dim(stamps, 1 - c, 1, 0)
    stamps_q = jnp.broadcast_to(mine, (8, HALF))
    stamps_k = jnp.broadcast_to(jnp.concatenate([mine, other], 1).reshape(L, 1), (L, 128))
    spaced = jnp.pad(patches.reshape(16, 2, IMG_GROUP, D), ((0, 0), (0, 0), (0, 2), (0, 0))).reshape(16, 64, D)
    words = lax.dynamic_slice_in_dim(text_features, t, 1, 0).reshape(8, 1, D)
    words = jnp.pad(words, ((0, 0), (IMG_GROUP, 1), (0, 0))).reshape(HALF, D)
    return (
        patch_weight.T,
        text_weight.T,
        heads_in_weight.transpose(0, 2, 3, 1).reshape(NL, 3 * DEV, D),
        heads_out_weight,
        up_weight,
        down_weight,
        vectors,
        gains,
        stamps_q,
        stamps_k,
        spaced,
        words,
    )


SUM_UNITS = [
    (256, 512, "z"),
    (256, 512, "y"),
    (256, 512, "z"),
    (256, 512, "y"),
    (256, 512, "z"),
    (256, 512, "y"),
    (0, 512, "z"),
]
NU = len(SUM_UNITS)
RING = 4
DOWN, UP, ATT, STEMS = 0, 1, 2, 6


class Sums:
    def __init__(self, grads, core_in, xr, pr, yr, qr, zb, tr, xs, ps, qs, fx, fp, out, send, recv, local, credit):
        self.grads, self.core_in = grads, core_in
        self.xr, self.pr, self.yr, self.qr, self.zb, self.tr = xr, pr, yr, qr, zb, tr
        self.xs, self.ps, self.qs, self.fx, self.fp = xs, ps, qs, fx, fp
        self.out, self.send, self.recv, self.local, self.credit = out, send, recv, local, credit

    def where(self, u):
        nx, npl, slow = SUM_UNITS[u]
        z, y, c, t = place()
        m = lambda v: pl.multiple_of(v, 16)
        fast = "y" if slow == "z" else "z"
        at = {"z": z, "y": y}
        return nx, npl, slow, fast, at, c, t, m

    def core(self, u):
        nx, npl, slow, fast, at, c, t, m = self.where(u)
        g, into = self.grads.at[u % 3], self.core_in.at[u % 2]
        out = []
        if nx:
            out.append(
                remote(
                    g.at[:, pl.ds(m((1 - c) * 128), 128)],
                    into.at[:, pl.ds(0, 128)],
                    self.send.at[u, 0],
                    self.recv.at[u, 0],
                    sibling(),
                )
            )
        out.append(
            remote(
                g.at[:, pl.ds(m(nx + (1 - c) * 256), 256)],
                into.at[:, pl.ds(128, 256)],
                self.send.at[u, 1],
                self.recv.at[u, 1],
                sibling(),
            )
        )
        return out

    def first(self, u):
        nx, npl, slow, fast, at, c, t, m = self.where(u)
        g = self.grads.at[u % 3]
        out = []
        for r in (1, 2, 3):
            if nx:
                out.append(
                    remote(
                        g.at[r, pl.ds(m(c * 128), 128)],
                        self.xr.at[u % RING, r - 1],
                        self.send.at[u, 1 + r],
                        self.recv.at[u, 1 + r],
                        peer("x", r),
                    )
                )
            block = (at[slow] + r) % 4
            out.append(
                remote(
                    g.at[:, pl.ds(m(nx + c * 256 + block * 64), 64)],
                    self.pr.at[u % RING, r - 1],
                    self.send.at[u, 4 + r],
                    self.recv.at[u, 4 + r],
                    peer(slow, r),
                )
            )
        return out

    def second(self, u):
        nx, npl, slow, fast, at, c, t, m = self.where(u)
        out = []
        for r in (1, 2, 3):
            if nx:
                block = (at["y"] + r) % 4
                out.append(
                    remote(
                        self.xs.at[u % 3, pl.ds(m(block * 32), 32)],
                        self.yr.at[u % RING, r - 1],
                        self.send.at[u, 7 + r],
                        self.recv.at[u, 7 + r],
                        peer("y", r),
                    )
                )
            block = (at[fast] + r) % 4
            out.append(
                remote(
                    self.ps.at[u % 3, :, pl.ds(m(block * 16), 16)],
                    self.qr.at[u % RING, r - 1],
                    self.send.at[u, 10 + r],
                    self.recv.at[u, 10 + r],
                    peer(fast, r),
                )
            )
        return out

    def third(self, u):
        nx, npl, slow, fast, at, c, t, m = self.where(u)
        out = []
        for r in (1, 2, 3):
            if nx:
                mine = self.zb.at[u % RING, at["z"]]
                out.append(remote(mine, mine, self.send.at[u, 13 + r], self.recv.at[u, 13 + r], peer("z", r)))
            out.append(
                remote(
                    self.qs.at[u % 3, r],
                    self.tr.at[u, r - 1],
                    self.send.at[u, 16 + r],
                    self.recv.at[u, 16 + r],
                    peer("x", r),
                )
            )
        return out

    def rows(self, u):
        nx, npl, slow, fast, at, c, t, m = self.where(u)
        base = u * D
        return (
            pl.ds(m(base + c * 128), 128),
            pl.ds(m(base + c * 128 + at["y"] * 32), 32),
            pl.ds(m(base + nx + c * 256), 256),
            pl.ds(m(base + nx + c * 256 + at[slow] * 64), 64),
            pl.ds(m(base + nx + c * 256 + at[slow] * 64 + at[fast] * 16), 16),
        )

    def fourth(self, u):
        nx, npl, slow, fast, at, c, t, m = self.where(u)
        _, x_own, _, _, p_own = self.rows(u)
        out = []
        for r in (1, 2, 3):
            if nx:
                out.append(
                    remote(
                        self.fx.at[u],
                        self.out.at[x_own],
                        self.send.at[u, 19 + r],
                        self.recv.at[u, 19 + r],
                        peer("y", r),
                    )
                )
            out.append(
                remote(
                    self.fp.at[u],
                    self.out.at[p_own],
                    self.send.at[u, 22 + r],
                    self.recv.at[u, 22 + r],
                    peer(fast, r),
                )
            )
        return out

    def own(self, u):
        nx = SUM_UNITS[u][0]
        _, x_own, _, _, p_own = self.rows(u)
        out = [pltpu.make_async_copy(self.fp.at[u], self.out.at[p_own], self.local.at[u, 0])]
        if nx:
            out.append(pltpu.make_async_copy(self.fx.at[u], self.out.at[x_own], self.local.at[u, 1]))
        return out

    def fifth(self, u):
        nx, npl, slow, fast, at, c, t, m = self.where(u)
        region = self.out.at[self.rows(u)[3]]
        return [
            remote(region, region, self.send.at[u, 25 + r], self.recv.at[u, 25 + r], peer(slow, r))
            for r in (1, 2, 3)
        ]

    def sixth(self, u):
        nx = SUM_UNITS[u][0]
        x_all, _, p_all, _, _ = self.rows(u)
        region = self.out.at[p_all]
        out = [remote(region, region, self.send.at[u, 29], self.recv.at[u, 29], sibling())]
        if nx:
            region = self.out.at[x_all]
            out.append(remote(region, region, self.send.at[u, 30], self.recv.at[u, 30], sibling()))
        return out

    def step(self, k, u):
        nx, npl, slow, fast, at, c, t, m = self.where(u)
        b, ring, rot = u % 3, u % RING, u % 3
        grads = self.grads
        if k == 0:
            if u >= 2:
                pl.semaphore_wait(self.credit, 1)
            for copy in self.core(u):
                copy.start()
        if k == 1:
            for copy in self.core(u):
                copy.wait_recv()
            parts = ([(0, 0, 128)] if nx else []) + [(nx, 128, 256)]
            for first, there, count in parts:

                def add(i, carry):
                    s = i // (count // 64)
                    o = (i % (count // 64)) * 64
                    mine = pl.ds(m(first + c * count + o), 64)
                    its = pl.ds(m(there + o), 64)
                    total = grads[b, s, mine].astype(F32) + self.core_in[u % 2, s, its].astype(F32)
                    grads[b, s, mine] = total.astype(BF)
                    return carry

                lax.fori_loop(0, 4 * (count // 64), add, 0)
            if u + 2 < NU:
                pl.semaphore_signal(self.credit, inc=1, device_id=sibling(), device_id_type=MESH)
            for copy in self.first(u):
                copy.start()
        if k == 2:
            for copy in self.first(u):
                copy.wait_recv()
            if nx:

                def addx(i, carry):
                    o = pl.ds(m(i * 32), 32)
                    total = grads[b, 0, pl.ds(m(c * 128 + i * 32), 32)].astype(F32)
                    for r in range(3):
                        total = total + self.xr[ring, r, o].astype(F32)
                    self.xs[rot, o] = total.astype(BF)
                    return carry

                lax.fori_loop(0, 4, addx, 0)

            def addp(i, carry):
                s = i // 2
                o = pl.ds(m((i % 2) * 32), 32)
                row = nx + c * 256 + at[slow] * 64 + (i % 2) * 32
                total = grads[b, s, pl.ds(m(row), 32)].astype(F32)
                for r in range(3):
                    total = total + self.pr[ring, r, s, o].astype(F32)
                self.ps[rot, s, o] = total.astype(BF)
                return carry

            lax.fori_loop(0, 8, addp, 0)
            for copy in self.core(u) + self.first(u):
                copy.wait_send()
            for copy in self.second(u):
                copy.start()
        if k == 3:
            for copy in self.second(u):
                copy.wait_recv()
            if nx:
                total = self.xs[rot, pl.ds(m(at["y"] * 32), 32)].astype(F32)
                for r in range(3):
                    total = total + self.yr[ring, r].astype(F32)
                self.zb[ring, at["z"]] = total.astype(BF)

            def addq(s, carry):
                total = self.ps[rot, s, pl.ds(m(at[fast] * 16), 16)].astype(F32)
                for r in range(3):
                    total = total + self.qr[ring, r, s].astype(F32)
                self.qs[rot, s] = total.astype(BF)
                return carry

            lax.fori_loop(0, 4, addq, 0)
            for copy in self.second(u):
                copy.wait_send()
            for copy in self.third(u):
                copy.start()
        if k == 4:
            for copy in self.third(u):
                copy.wait_recv()
            if nx:
                total = self.zb[ring, 0].astype(F32)
                for r in (1, 2, 3):
                    total = total + self.zb[ring, r].astype(F32)
                self.fx[u] = total.astype(BF)
            total = self.qs[rot, 0].astype(F32)
            for r in range(3):
                total = total + self.tr[u, r].astype(F32)
            self.fp[u] = total.astype(BF)
            for copy in self.third(u):
                copy.wait_send()
            for copy in self.own(u) + self.fourth(u):
                copy.start()
        if k == 5:
            for copy in self.fourth(u):
                copy.wait_recv()
            for copy in self.own(u):
                copy.wait()
            for copy in self.fifth(u):
                copy.start()
        if k == 6:
            for copy in self.fifth(u):
                copy.wait_recv()
            for copy in self.sixth(u):
                copy.start()
        if k == 7:
            for copy in self.sixth(u):
                copy.wait_recv()
            for copy in self.fourth(u) + self.fifth(u) + self.sixth(u):
                copy.wait_send()


def norm_back(x, grad, base, gain, out, sums, gain_row, shift_row):
    zero = jnp.zeros((1, D), F32)
    sums[gain_row : gain_row + 1] = zero
    sums[shift_row : shift_row + 1] = zero

    def body(rows):
        v = x[rows]
        g = grad[rows]
        mean = jnp.mean(v, axis=-1, keepdims=True)
        centred = v - mean
        spread = jnp.mean(centred * centred, axis=-1, keepdims=True)
        inv = lax.rsqrt(spread + EPS)
        hat = centred * inv
        sums[gain_row : gain_row + 1] += jnp.sum(g * hat, axis=0, keepdims=True)
        sums[shift_row : shift_row + 1] += jnp.sum(g, axis=0, keepdims=True)
        d = g * gain
        first = jnp.mean(d, axis=-1, keepdims=True)
        second = jnp.mean(d * hat, axis=-1, keepdims=True)
        out[rows] = base[rows] + inv * (d - first - hat * second)

    row_blocks(32, body)


def returns(act, act_out, pgs, pg_out, tgs, tg_out, send, recv, own, mode, which):
    z, y, c, t = place()
    d = z * 4 + y
    if which == 0:
        for r in (1, 2, 3):
            a = (t + r) % 4
            copy = remote(act.at[a], act_out.at[t], send.at[r], recv.at[r], (d, c, a))
            copy.start() if mode == "start" else copy.wait()
        copy = pltpu.make_async_copy(act.at[t], act_out.at[t], own.at[0])
        copy.start() if mode == "start" else copy.wait()
        return
    for r in (1, 2, 3):
        a = (t + r) % 4
        copy = remote(tgs.at[a], tg_out.at[t], send.at[4 + r], recv.at[4 + r], (d, c, a))
        copy.start() if mode == "start" else copy.wait()
    copy = pltpu.make_async_copy(tgs.at[t], tg_out.at[t], own.at[1])
    copy.start() if mode == "start" else copy.wait()

    def each(i, carry):
        a, yy = i % 4, i // 4
        to_me = (t == z) & (yy == y) & (a == t)
        src = pgs.at[a, pl.ds(pl.multiple_of(yy * 64, 64), 64)]
        local = pltpu.make_async_copy(src, pg_out.at[d], own.at[2])
        away = remote(src, pg_out.at[d], send.at[8 + i], recv.at[8 + d], (t * 4 + yy, c, a))

        @pl.when(to_me)
        def _():
            local.start() if mode == "start" else local.wait()

        @pl.when(jnp.logical_not(to_me))
        def _():
            away.start() if mode == "start" else away.wait_send()

        return carry

    lax.fori_loop(0, 16, each, 0)
    if mode == "wait":

        def arrive(i, carry):
            from_me = (t == z) & (i == d)

            @pl.when(jnp.logical_not(from_me))
            def _():
                remote(pg_out.at[i], pg_out.at[i], send.at[8 + i], recv.at[8 + i], (i, c, z)).wait_recv()

            return carry

        lax.fori_loop(0, 16, arrive, 0)


def backward_kernel(
    w_in,
    patch_in,
    xs_in,
    mid_in,
    nrm_in,
    fn_in,
    tri_in,
    kvo_in,
    mix_in,
    lse_in,
    pre_in,
    act_in,
    gains,
    stamps_q,
    stamps_k,
    words,
    cotangent,
    row_scale,
    out,
    act_out,
    pg_out,
    tg_out,
    wb,
    gain,
    stamp_q,
    stamp_k,
    prow,
    word,
    cot,
    rscale,
    xs,
    mid,
    nrm,
    fn,
    tri,
    kvo,
    mix,
    lse,
    pre,
    bias,
    up,
    low,
    back,
    hgrad,
    hid,
    pgrad,
    fnt,
    kvg,
    kvs,
    rkv,
    tgrad,
    sums,
    vec,
    pgs,
    tgs,
    grads,
    core_in,
    xr,
    pr,
    yr,
    qr,
    zb,
    tr,
    sxs,
    sps,
    sqs,
    fx,
    fp,
    wsem,
    lsem,
    send,
    recv,
    local,
    credit,
    ksend,
    krecv,
    rsend,
    rrecv,
    rown,
):
    z, y, c, t = place()
    copy_in = pltpu.make_async_copy

    def section(row, rows, s):
        return copy_in(w_in.at[s, pl.ds(row, rows)], wb.at[s, pl.ds(0, rows)], wsem.at[s])

    sections = []
    for which in (1, 0):
        base = STEM + which * LAYER
        sections += [(base + 1536, 768), (base + 768, 768), (base, 768)]
    sections.append((0, STEM))

    def acts(which):
        return [
            copy_in(pre_in.at[which], pre, lsem.at[0]),
            copy_in(fn_in.at[which], fn, lsem.at[1]),
            copy_in(mid_in.at[which], mid, lsem.at[2]),
            copy_in(tri_in.at[which], tri, lsem.at[3]),
            copy_in(kvo_in.at[which], kvo, lsem.at[4]),
            copy_in(mix_in.at[which], mix, lsem.at[5]),
            copy_in(lse_in.at[which], lse, lsem.at[6]),
            copy_in(nrm_in.at[which], nrm, lsem.at[7]),
            copy_in(xs_in.at[which], xs, lsem.at[8]),
        ]

    head = [
        copy_in(cotangent.at[t], cot, lsem.at[9]),
        copy_in(row_scale, rscale, lsem.at[10]),
    ]
    for copy in head:
        copy.start()
    for s in range(4):
        section(*sections[0], s).start()
    loads = acts(1)
    for copy in loads:
        copy.start()
    rest = [
        copy_in(gains, gain, lsem.at[11]),
        copy_in(stamps_q, stamp_q, lsem.at[12]),
        copy_in(stamps_k, stamp_k, lsem.at[13]),
        copy_in(patch_in, prow, lsem.at[14]),
        copy_in(words, word, lsem.at[15]),
    ]
    for copy in rest:
        copy.start()
    greet("out")
    returns(act_in, act_out, pgs, pg_out, tgs, tg_out, rsend, rrecv, rown, "start", 0)
    total = Sums(
        grads, core_in, xr, pr, yr, qr, zb, tr, sxs, sps, sqs, fx, fp, out, send, recv, local, credit
    )

    def comm(*steps):
        for k, u in steps:
            total.step(k, u)

    for copy in head:
        copy.wait()

    def first_up(rows):
        up[rows] = cot[rows].astype(F32) * rscale[rows, 0:1]

    row_blocks(64, first_up)
    vec[...] = jnp.zeros_like(vec)
    sums[...] = jnp.zeros_like(sums)
    for copy in rest:
        copy.wait()

    def see(i, carry):
        rows = pl.ds(pl.multiple_of(i * 64, 64), 64)
        bias[rows] = jnp.where(stamp_k[rows, 0:1] <= stamp_q[0:1, :], 0.0, MASKED)
        return carry

    lax.fori_loop(0, 8, see, 0)

    plan = {
        (1, "down"): [(0, 0)],
        (1, "up"): [(1, 0), (0, 1)],
        (1, "att1"): [(1, 1)],
        (1, "att2"): [(2, 0)],
        (1, "in"): [(0, 2), (2, 1), (3, 0)],
        (0, "down"): [(0, 3), (1, 2), (3, 1), (4, 0)],
        (0, "up"): [(2, 2), (0, 4), (1, 3), (4, 1), (5, 0)],
        (0, "att1"): [(6, 0), (1, 4), (2, 3), (3, 2), (5, 1)],
        (0, "att2"): [(6, 1), (4, 2), (3, 3)],
        (0, "in"): [(0, 5), (2, 4), (1, 5), (5, 2)],
    }
    for which in (1, 0):
        u0 = 0 if which else 3
        loads = acts(which)
        loads[0].wait()

        def round_up(rows):
            low[rows] = up[rows].astype(BF)

        row_blocks(64, round_up)
        b = u0 % 3
        after = sections[u0 + 1]

        def down(s, carry):
            section(*sections[u0], s).wait()
            hgrad[...] = dot_nt(low[...], wb[s])
            section(*after, s).start()

            def body(rows):
                x = pre[s, rows]
                th = jnp.tanh(GELU_A * (x + GELU_B * x * x * x))
                hid[rows] = (0.5 * x * (1.0 + th)).astype(BF)
                slope = 0.5 * (1.0 + th) + 0.5 * x * (1.0 - th * th) * (GELU_A * (1.0 + 3.0 * GELU_B * x * x))
                pgrad[s, rows] = (hgrad[rows] * slope).astype(BF)

            row_blocks(32, body)
            for j in range(3):
                grads[b, s, 256 * j : 256 * j + 256] = dot_tn(hid[:, 256 * j : 256 * j + 256], low[...]).astype(BF)
            vec[s, which : which + 1] = jnp.sum(pgrad[s].astype(F32), axis=0, keepdims=True)
            return carry

        lax.fori_loop(0, 4, down, 0)
        if which:
            acts(0)[0].start()
        comm(*plan[which, "down"])

        b = (u0 + 1) % 3
        after = sections[u0 + 2]
        loads[1].wait()
        fnt[...] = fn[...].T
        back[...] = jnp.zeros_like(back)

        def lift(s, carry):
            section(*sections[u0 + 1], s).wait()
            back[...] += dot_nt(pgrad[s], wb[s])
            section(*after, s).start()
            for j in range(3):
                grads[b, s, 256 * j : 256 * j + 256] = dot_nn(fnt[256 * j : 256 * j + 256], pgrad[s]).astype(BF)
            return carry

        lax.fori_loop(0, 4, lift, 0)
        if which:
            acts(0)[1].start()
        comm(*plan[which, "up"])

        loads[2].wait()
        norm_back(mid, back, up, gain[4 + which : 5 + which], up, sums, 6 + which, 8 + which)
        if which:
            acts(0)[2].start()
        row_blocks(64, round_up)
        for k in (3, 4, 5, 6):
            loads[k].wait()
        b = (u0 + 2) % 3
        after = sections[u0 + 3]

        def share(s):
            return remote(kvs.at[which, s], rkv.at[which, s], ksend.at[which, s], krecv.at[which, s], sibling())

        def attend(s, carry):
            section(*sections[u0 + 2], s).wait()
            grads[b, s, 576:768] = dot_nn(mix[s], low[...]).astype(BF)
            mixed = dot_nt(wb[s, 576:768], low[...]).astype(BF)
            for h in range(3):
                at = 64 * h
                q = tri[s, at : at + 64] * jnp.asarray(HEAD_DIM**-0.5, BF)
                do = mixed[at : at + 64]
                k1, v1 = tri[s, 192 + at : 256 + at], tri[s, 384 + at : 448 + at]
                k2, v2 = kvo[s, at : at + 64], kvo[s, 192 + at : 256 + at]
                log_total = lse[s, h : h + 1]
                p1 = jnp.exp(dot_tn(k1, q) + bias[0:256] - log_total)
                p2 = jnp.exp(dot_tn(k2, q) + bias[256:512] - log_total)
                d1 = dot_tn(v1, do)
                d2 = dot_tn(v2, do)
                delta = jnp.sum(p1 * d1, axis=0, keepdims=True) + jnp.sum(p2 * d2, axis=0, keepdims=True)
                g1 = (p1 * (d1 - delta)).astype(BF)
                g2 = (p2 * (d2 - delta)).astype(BF)
                dq = (dot_nn(k1, g1) + dot_nn(k2, g2)) * HEAD_DIM**-0.5
                tgrad[s, at : at + 64] = dq.astype(BF)
                kvg[s, at : at + 64] = dot_nt(q, g1)
                kvs[which, s, at : at + 64] = dot_nt(q, g2).astype(BF)
                kvg[s, 192 + at : 256 + at] = dot_nt(do, p1.astype(BF))
                kvs[which, s, 192 + at : 256 + at] = dot_nt(do, p2.astype(BF)).astype(BF)
            share(s).start()
            return carry

        lax.fori_loop(0, 2, attend, 0)
        comm(*plan[which, "att1"])
        lax.fori_loop(2, 4, attend, 0)
        if which:
            for k in (3, 4, 5, 6):
                acts(0)[k].start()
        comm(*plan[which, "att2"])
        loads[7].wait()
        back[...] = jnp.zeros_like(back)

        def lead(s, carry):
            share(s).wait_recv()
            tgrad[s, 192:576] = (kvg[s] + rkv[which, s].astype(F32)).astype(BF)
            grads[b, s, 0:576] = dot_nn(tgrad[s], nrm[...]).astype(BF)
            back[...] += dot_tn(tgrad[s], wb[s, 0:576])
            section(*after, s).start()
            return carry

        lax.fori_loop(0, 4, lead, 0)
        if which:
            acts(0)[7].start()
        comm(*plan[which, "in"])
        loads[8].wait()
        norm_back(xs, back, up, gain[which : which + 1], up, sums, 2 + which, 4 + which)
        if which:
            acts(0)[8].start()

    row_blocks(64, round_up)
    place_in = lax.broadcasted_iota(jnp.int32, (HALF, 1), 0) % (IMG_GROUP + 2)
    rounded = low[...].astype(F32)
    sums[10:11] = jnp.sum(jnp.where(place_in < IMG_GROUP, rounded, 0.0), axis=0, keepdims=True)
    sums[11:12] = jnp.sum(jnp.where(place_in == IMG_GROUP, rounded, 0.0), axis=0, keepdims=True)
    sums[12:13] = jnp.sum(jnp.where(place_in > IMG_GROUP, up[...], 0.0), axis=0, keepdims=True)
    fnt[...] = low[...].T
    b = STEMS % 3
    back[...] = jnp.zeros_like(back)
    hgrad[...] = jnp.zeros_like(hgrad)
    for a in range(4):
        s = (a - t) % 4
        section(*sections[6], s).wait()
        mine = fnt[192 * a : 192 * a + 192]
        grads[b, s, 0:192] = dot_nn(mine, prow[...].reshape(HALF, D)).astype(BF)
        grads[b, s, 192:384] = dot_nn(mine, word[...]).astype(BF)
        vec[s, 2:16] = sums[2:16]
        grads[b, s, 384:400] = vec[s].astype(BF)
        grads[b, s, 400:512] = jnp.zeros((112, D), BF)
        back[...] += dot_tn(mine, wb[s, 0:192])
        hgrad[...] += dot_tn(mine, wb[s, 192:384])
    comm((0, 6))
    for a in range(4):
        pgs[a] = back[:, 192 * a : 192 * a + 192].astype(BF)
    for h in range(8):
        row = hgrad[32 * h + 30 : 32 * h + 31]
        for a in range(4):
            tgs[a, h : h + 1] = row[:, 192 * a : 192 * a + 192]
    returns(act_in, act_out, pgs, pg_out, tgs, tg_out, rsend, rrecv, rown, "start", 1)
    comm((6, 2), (4, 3), (3, 4), (2, 5), (1, 6), (5, 3), (4, 4), (3, 5), (2, 6), (6, 3), (5, 4), (4, 5), (3, 6))
    comm((6, 4), (5, 5), (4, 6), (6, 5), (5, 6), (6, 6))
    returns(act_in, act_out, pgs, pg_out, tgs, tg_out, rsend, rrecv, rown, "wait", 0)
    returns(act_in, act_out, pgs, pg_out, tgs, tg_out, rsend, rrecv, rown, "wait", 1)
    for which in range(NL):
        for s in range(4):
            remote(kvs.at[which, s], rkv.at[which, s], ksend.at[which, s], krecv.at[which, s], sibling()).wait_send()
    for u in range(NU):
        total.step(7, u)


def backward_call(*args):
    any_ = pl.BlockSpec(memory_space=pl.ANY)
    sds = jax.ShapeDtypeStruct
    dma = pltpu.SemaphoreType.DMA
    v = pltpu.VMEM
    return pl.pallas_call(
        backward_kernel,
        out_shape=(
            sds((6 * D + 512, D), BF),
            sds((4, 192, HALF), BF),
            sds((16, 64, 192), BF),
            sds((4, 8, 192), F32),
        ),
        in_specs=[any_] * 18,
        out_specs=(any_,) * 4,
        scratch_shapes=[
            v((4, D, D), BF),
            v((8, D), F32),
            v((8, HALF), jnp.int32),
            v((L, 128), jnp.int32),
            v((4, 64, D), BF),
            v((HALF, D), BF),
            v((HALF, D), BF),
            v((HALF, 128), F32),
            v((HALF, D), F32),
            v((HALF, D), F32),
            v((HALF, D), BF),
            v((HALF, D), BF),
            v((4, 576, HALF), BF),
            v((4, 384, HALF), BF),
            v((4, 192, HALF), BF),
            v((4, 8, HALF), F32),
            v((4, HALF, D), F32),
            v((L, HALF), F32),
            v((HALF, D), F32),
            v((HALF, D), BF),
            v((HALF, D), F32),
            v((HALF, D), F32),
            v((HALF, D), BF),
            v((4, HALF, D), BF),
            v((D, HALF), BF),
            v((4, 384, HALF), F32),
            v((2, 4, 384, HALF), BF),
            v((2, 4, 384, HALF), BF),
            v((4, 576, HALF), BF),
            v((16, D), F32),
            v((4, 16, D), F32),
            v((4, HALF, DEV), BF),
            v((4, 8, DEV), F32),
            v((3, 4, D, D), BF),
            v((2, 4, 384, D), BF),
            v((RING, 3, 128, D), BF),
            v((RING, 3, 4, 64, D), BF),
            v((RING, 3, 32, D), BF),
            v((RING, 3, 4, 16, D), BF),
            v((RING, 4, 32, D), BF),
            v((NU, 3, 16, D), BF),
            v((3, 128, D), BF),
            v((3, 4, 64, D), BF),
            v((3, 4, 16, D), BF),
            v((NU, 32, D), BF),
            v((NU, 16, D), BF),
            dma((4,)),
            dma((16,)),
            dma((NU, 31)),
            dma((NU, 31)),
            dma((NU, 2)),
            pltpu.SemaphoreType.REGULAR,
            dma((2, 4)),
            dma((2, 4)),
            dma((24,)),
            dma((24,)),
            dma((3,)),
        ],
        compiler_params=pltpu.CompilerParams(
            collective_id=1, has_side_effects=True, vmem_limit_bytes=63 * 2**20
        ),
    )(*args)


def shards(*args):
    (datasets, dataset_weights, action_mask, cotangent) = args[17:]
    t = lax.axis_index("tensor")
    ops = prepare(*args[:17])
    gains, stamps_q, stamps_k, words = ops[7], ops[8], ops[9], ops[11]
    kept = forward_call(*ops)
    mask = lax.dynamic_slice_in_dim(action_mask, t, 1, 0)[0]
    dataset = lax.dynamic_slice_in_dim(datasets, t, 1, 0)[0]
    weight = jnp.sum(jnp.where(jnp.arange(dataset_weights.shape[0]) == dataset, dataset_weights, 0))
    scale = weight.astype(F32) * mask.astype(F32)
    last = jnp.arange(IMG_GROUP + 2) == IMG_GROUP + 1
    row_scale = jnp.where(last[None, :], scale[:, None], 1.0).reshape(HALF, 1)
    row_scale = jnp.broadcast_to(row_scale, (HALF, 128))
    out, act, pg, tg = backward_call(
        kept[0], kept[1], *kept[3:], gains, stamps_q, stamps_k, words, cotangent, row_scale
    )
    part = lambda u, a, b: out[u * D + a : u * D + b].astype(F32)
    heads_in = jnp.stack([part(5, 0, 576), part(2, 0, 576)]).reshape(NL, 3, DEV, D).transpose(0, 3, 1, 2)
    heads_out = jnp.stack([part(5, 576, 768), part(2, 576, 768)])
    up_grad = jnp.stack([part(4, 0, 768), part(1, 0, 768)])
    down_grad = jnp.stack([part(3, 0, 768), part(0, 0, 768)])
    vectors = part(6, 384, 400)
    own = lax.dynamic_slice_in_dim(vectors, t * DEV, DEV, 1)
    pg = pg.reshape(16, 2, IMG_GROUP + 2, DEV)[:, :, :IMG_GROUP].reshape(960, DEV).astype(F32)
    return (
        act.transpose(0, 2, 1),
        pg,
        tg,
        part(6, 0, 192).T,
        own[10],
        part(6, 192, 384).T,
        own[11],
        own[12],
        own[2:4],
        own[4:6],
        heads_in,
        heads_out,
        own[6:8],
        own[8:10],
        up_grad,
        vectors[0:2],
        down_grad,
    )


def solution(mesh):
    in_specs = (
        P(("dp", "ctx"), None),
        P("dp", "ctx", None),
        P(None, "tensor"),
        P("tensor"),
        P(None, "tensor"),
        P("tensor"),
        P("tensor"),
        P(),
        P(),
        P(None, None, None, "tensor"),
        P(None, "tensor", None),
        P(),
        P(),
        P(None, None, "tensor"),
        P(None, "tensor"),
        P(None, "tensor", None),
        P("dp", None),
        P("dp"),
        P(),
        P("dp", "ctx"),
        P("dp", "ctx", None),
    )
    out_specs = (
        P("dp", "ctx", "tensor"),
        P(("dp", "ctx"), "tensor"),
        P("dp", "ctx", "tensor"),
        P(None, "tensor"),
        P("tensor"),
        P(None, "tensor"),
        P("tensor"),
        P("tensor"),
        P(None, "tensor"),
        P(None, "tensor"),
        P(None, None, None, "tensor"),
        P(None, "tensor", None),
        P(None, "tensor"),
        P(None, "tensor"),
        P(None, None, "tensor"),
        P(None, "tensor"),
        P(None, "tensor", None),
    )
    return jax.shard_map(shards, mesh=mesh, in_specs=in_specs, out_specs=out_specs, check_vma=False)
```

time: 886 us -> 379 us (0.43); the launches traced: 876 us -> 378 us
  waiting for transfers between devices: 420 us -> 0 us
  Pallas kernels: 0 us -> 345 us
  blocking collectives: 119 us -> 0 us
  matrix products: 113 us -> 0 us
  local copies, waits for them, and re-layouts: 103 us -> 17.6 us
  other arithmetic: 96.3 us -> 14.1 us
  between operations: 16.4 us -> 1.53 us
    psum x8 -> x0, waiting for transfers between devices: 407 us -> none  [the longest x2 107 us: shards(): lax.psum(layer_feed_terms.astype(jnp.bfloat16), 'tensor')]
    pallas_call x0 -> x2, Pallas kernels: none -> 345 us  [the longest x1 202 us: backward_call(): pl.pallas_call(backward_kernel, out_shape=(sds((6 * D + 512, D), BF), sds...]
    dot_general x40 -> x0, matrix products: 107 us -> none  [the longest x4 12.8 us: mix_values(): jnp.einsum('bhqk,bkhd->bqhd', probs_low, split_heads(values_all, L), pref...]
    psum x1 -> x0, blocking collectives: 66.6 us -> none  [shards(): lax.psum(patch_bias_gradient.astype(jnp.bfloat16), ('dp', 'ctx'))]
    reduce_sum x22 -> x1, other arithmetic: 40.5 us -> 1.28 us  [shards(): jnp.sum(jnp.where(jnp.arange(dataset_weights.shape[0]) == dataset, datase...]
    convert_element_type x26 -> x2, other arithmetic: 38.4 us -> 0.86 us  [the longest x1 0.74 us: shards(): part = lambda u, a, b: out[u * D + a:u * D + b].astype(F32)]
    unnamed x202 -> x26, local copies, waits for them, and re-layouts: 35.2 us -> 2.65 us
    another operation x25 -> x1, local copies, waits for them, and re-layouts: 34.1 us -> 2.64 us  [shards(): down_grad = jnp.stack([part(3, 0, 768), part(0, 0, 768)])]
  transfers between devices with their start and end apart: 16 -> 0, of which waited for: 11 -> 0; matrix products, arithmetic and copies ran while one was open for 14% -> 0% of each run, Pallas kernels for 0% -> 0%
where the time goes in v1:
time: 379 us; the launch traced here: 378 us
  Pallas kernels  345 us (91%)
  local copies, waits for them, and re-layouts  17.6 us (5%)
  other arithmetic  14.1 us (4%)
    pallas_call x1, Pallas kernels, backward_call(): pl.pallas_call(backward_kernel, out_shape=(sds((6 * D + 512, D), BF), sds...  202 us
    pallas_call x1, Pallas kernels, forward_call(): pl.pallas_call(gather_kernel, out_shape=tuple((sds(s, d) for s, d in shap...  143 us

profile of v1, /device:TPU:1, one launch (start us, length us, event | category | flops | bytes accessed | tf_op | source)
XLA Modules:
  0.0 378.4 jit_solution(10542517104186801434)
XLA Ops:
  0.7 0.0 copy-start
  0.7 0.7 dynamic-slice_reduce_fusion
  1.4 0.8 broadcast_in_dim.68.stamps_k
  2.3 0.6 broadcast_in_dim.66.stamps_q
  2.9 0.0 copy-done
  2.9 0.8 pad.23.clone
  3.7 1.4 pad_maximum_fusion.gains
  5.1 2.3 reshape.98
  7.4 0.0 copy-start.6
  7.4 0.0 copy-start.7
  7.4 0.0 copy-start.8
  7.4 0.0 copy-start.5
  7.4 1.4 pad.22
  8.8 0.0 copy-done.6
  8.8 0.0 copy-done.7
  8.8 0.0 copy-done.8
  8.9 0.0 copy-done.5
  8.9 0.6 concatenate.11.vectors
  9.5 0.0 copy-start.9
  9.5 0.0 copy-start.10
  9.5 142.8 %shard_map.332 = (bf16[4,4992,768]{2,1,0:T(8,128)(2,1)}, bf16[4,64,768]{2,1,0:T(8,128)(2,1)}, f32[4,8,768]{2,1,0:T(8,128)}, f32[2,256,768]{2,1,0:T(8,128)}, f32[...) custom-call(bf16[192,768]{1,0:T(8,128)(2,1)} %bitcast.47, ...), custom_call_target="tpu_custom_call" | custom-call | tf_op jit(solution)/shard_map/pallas_call | solution.py:503
  152.3 0.0 copy-done.9
  152.3 0.6 dynamic_slice.25
  152.9 0.0 copy-done.10
  152.9 1.3 fusion.3
  154.8 0.7 fusion.2
  155.5 0.1 broadcast_select_fusion
  155.6 0.1 select_n.35
  155.7 0.8 broadcast_in_dim.73.row_scale
  156.5 202.4 %shard_map.333 = (bf16[5120,768]{1,0:T(8,128)(2,1)}, bf16[4,192,256]{2,1,0:T(8,128)(2,1)}, bf16[16,64,192]{2,1,0:T(8,128)(2,1)}, f32[4,8,192]{2,1,0:T(8,128)}) custom-call(bf16[4,4992,768]{2,1,0:T(8,128)(2,1)} %get-tuple-element.33.w_in, bf16[4,64,768]{2,1,0:T(8,128)(2,1)} %get-tuple-element.34.patch_in, f32[2,256,768]{2,1,0:T(8,128)} %get-tuple-element.35.xs_in, ...), custom_call_target="tpu_custom_call" | custom-call | tf_op jit(solution)/shard_map/pallas_call | solution.py:1307
  358.9 2.6 slice_bitcast_fusion.1
  361.5 4.3 %maximum_convert_fusion = (f32[2,768,768]{2,1,0:T(8,128)}, f32[2,768,768]{2,1,0:T(8,128)}) fusion(bf16[1,768,768]{2,1,0:T(8,128)(2,1)S(1)} %get-tuple-element.68, bf16[1,768,768]{2,1,0:T(8,128)(2,1)S(1)} %get-tuple-element.69, bf16[1,768,768]{2,1,0:T(8,128)(2,1)S(1)} %get-tuple-element.67, bf16[1,768,768]{2,1,0:T(8,128)(2,1)S(1)} %get-tuple-element.66), kind=kLoop, calls=%fused_computation.1 | loop fusion | flops 4718592 | bytes 14155776 | tf_op jit(solution)/shard_map/stack | solution.py:1401
  365.9 2.4 slice_bitcast_fusion.5
  368.2 1.1 maximum_convert_fusion.2
  369.3 1.5 fusion.4
  370.9 0.0 copy-start.2
  370.9 2.0 convert_bitcast_fusion
  372.9 0.0 copy-done.2
  372.9 0.1 slice_convert_fusion
  373.0 0.0 copy-start.3
  373.1 0.0 copy-start.1
  373.1 0.1 reshape.104
  373.2 0.0 copy-start.4
  373.2 1.2 copy.40
  374.4 0.7 slice_convert_fusion.1
  375.1 0.7 fusion.5
  375.8 0.6 fusion.6
  376.5 0.6 slice.81
  377.1 0.0 copy-done.3
  377.1 0.7 copy.44
  377.8 0.0 copy-done.4
  377.8 0.6 copy.45
  378.4 0.0 copy-done.1
  (13 shorter events, 0.1 us)
Async XLA Ops:
  0.7 2.2 copy-start
  7.4 1.4 copy-start.6
  7.4 1.4 copy-start.7
  7.4 1.4 copy-start.8
  7.4 1.5 copy-start.5
  9.5 142.8 %copy-start.9 = (s32[4]{0:T(128)S(1)}, s32[4]{0:T(128)}, u32[]{:S(2)}) copy-start(s32[4]{0:T(128)} %param.38) | copy-start | bytes 52
  9.5 143.4 %copy-start.10 = (s32[25]{0:T(128)S(1)}, s32[25]{0:T(128)}, u32[]{:S(2)}) copy-start(s32[25]{0:T(128)} %param.39) | copy-start | bytes 304
  370.9 2.0 copy-start.2
  373.0 4.0 %copy-start.3 = (bf16[4,192,256]{2,1,0:T(8,128)(2,1)S(1)}, bf16[4,192,256]{2,1,0:T(8,128)(2,1)}, u32[]{:S(2)}) copy-start(bf16[4,192,256]{2,1,0:T(8,128)(2,1)} %get-tuple-element.45) | copy-start | bytes 1179652
  373.1 5.4 %copy-start.1 = (bf16[4,8,768]{2,1,0:T(8,128)(2,1)S(1)}, bf16[4,8,768]{2,1,0:T(8,128)(2,1)}, u32[]{:S(2)}) copy-start(bf16[4,8,768]{2,1,0:T(8,128)(2,1)} %param.22) | copy-start | bytes 147460
  373.2 4.6 %copy-start.4 = (f32[4,8,192]{2,1,0:T(8,128)S(1)}, f32[4,8,192]{2,1,0:T(8,128)}, u32[]{:S(2)}) copy-start(f32[4,8,192]{2,1,0:T(8,128)} %get-tuple-element.106) | copy-start | bytes 73732
